TPU v7x, 32 devices: a whole 2x2x4 slice. The times are simulated.
32 devices in a mesh: grp: 2 (over x), tm: 16 (over z, y, core).
Axes of the slice: x: 2, y: 2, z: 4, core: 2. Of those that a mesh axis runs over, the one named last changes fastest.
Arguments:
- observations: bfloat16 [65536, 1024], P(('grp', 'tm')), parts along dimension 0, may hold values from -0.1875 to 0.1875
- counts: int32 [32], P(('grp', 'tm')), parts along dimension 0, may hold values from 1 to 2048, 10922 in all
- prior: float32 [32, 1024], P(('grp', 'tm')), parts along dimension 0, may hold values from 0.5 to 4
Outputs:
- factors: float32 [32, 1024, 1024], P(('grp', 'tm')), parts along dimension 0
There are 2 independent parts, one for each index of `grp`. A program takes and returns all parts, laid end to end along the dimension named above; each array names one. Nothing has to cross between parts.
Inputs may be any that keep to these rules, and one draw needn't show every extreme that they name: `counts`: some step has exactly 2048 live rows in every draw.
All inputs are finite; a program needn't handle non-finite values. No bound on the sum of `counts` on one device may be relied on, other than what follows from the above.
Results may differ from a plain program's by a relative error of at most 0.0003.
Values sent between devices are 32-bit elements; how exact they have to be, the bound alone decides.
A program may use at most 64 MiB of HBM per device.

v0:
```python
import jax
import jax.numpy as jnp
from jax import lax
from jax.sharding import PartitionSpec as P


def from_behind(block, axis, distance):
    devices = range(lax.axis_size(axis))
    route = [(i - distance, i) for i in devices if i - distance in devices]
    return lax.ppermute(block, axis, route)


def row_gram(block_rows):
    return lax.dot_general(
        block_rows, block_rows, (((0,), (0,)), ((), ())), preferred_element_type=jnp.float32
    )


def square_back(lower_factor):
    return lax.dot_general(
        lower_factor,
        lower_factor,
        (((1,), (1,)), ((), ())),
        precision=lax.Precision.HIGHEST,
        preferred_element_type=jnp.float32,
    )


def split_cholesky(matrix):
    order = matrix.shape[0]
    half = order // 2
    lead_block = jnp.linalg.cholesky(matrix[:half, :half])
    side_block = jax.scipy.linalg.solve_triangular(lead_block, matrix[half:, :half].T, lower=True).T
    trailing = matrix[half:, half:] - square_back(side_block)
    tail_block = jnp.linalg.cholesky(trailing)
    upper_rows = jnp.concatenate([lead_block, jnp.zeros((half, order - half), matrix.dtype)], 1)
    lower_rows = jnp.concatenate([side_block, tail_block], 1)
    return jnp.concatenate([upper_rows, lower_rows], 0)


def body(observations, counts, prior):
    capacity, columns = observations.shape
    live_count = counts[0]
    row_index = lax.broadcasted_iota(jnp.int32, (capacity, 1), 0)
    masked = jnp.where(row_index < live_count, observations, jnp.zeros_like(observations))
    gram_matrix = row_gram(masked)
    gram_matrix = gram_matrix + jnp.diag(prior[0])
    level_one = gram_matrix + from_behind(gram_matrix, "tm", 1)
    level_two = level_one + from_behind(level_one, "tm", 2)
    upper_factor = split_cholesky(level_two).T
    return upper_factor[None]


def solution(mesh):
    placed = (P(("grp", "tm"), None), P(("grp", "tm")), P(("grp", "tm"), None))
    return jax.shard_map(
        body, mesh=mesh, in_specs=placed, out_specs=P(("grp", "tm"), None, None), check_vma=False
    )
```

profile of v0, /device:TPU:24, one launch (start us, length us, event | category | flops | bytes accessed | tf_op | source)
XLA Modules:
  0.0 417.1 jit_solution(13306791997504786718)
XLA Ops:
  0.7 8.5 %select_add_fusion = f32[1024,1024]{0,1:T(8,128)S(1)} fusion(f32[1024]{0:T(1024)} %bitcast.76, bf16[2048,1024]{1,0:T(8,128)(2,1)} %param.4, pred[2048]{0:T(1024)(128)(4,1)S(1)} %iota_compare_fusion.5), kind=kOutput, calls=%fused_computation.5 | convolution fusion | flops 4300210176 | bytes 8394752 | tf_op jit(solution)/shard_map/dot_general | solution.py:14
  11.1 48.8 %collective-permute-done = f32[1024,1024]{0,1:T(8,128)S(1)} collective-permute-done((f32[1024,1024]{0,1:T(8,128)S(1)}, f32[1024,1024]{0,1:T(8,128)S(1)}, u32[]{:S(2)}, u32[]{:S(2)}) %collective-permute-start) | collective-permute-done | bytes 4194336 | tf_op jit(solution)/shard_map/ppermute | solution.py:10
  59.9 2.9 add.45
  65.6 91.1 %collective-permute-done.1 = f32[1024,1024]{0,1:T(8,128)} collective-permute-done((f32[1024,1024]{0,1:T(8,128)}, f32[1024,1024]{0,1:T(8,128)}, u32[]{:S(2)}, u32[]{:S(2)}) %collective-permute-start.1) | collective-permute-done | bytes 4194336 | tf_op jit(solution)/shard_map/ppermute | solution.py:10
  156.7 4.4 %add.46 = f32[1024,1024]{0,1:T(8,128)S(1)} add(f32[1024,1024]{0,1:T(8,128)} %add.45, f32[1024,1024]{0,1:T(8,128)} %collective-permute-done.1) | non-fusion elementwise | flops 1048576 | bytes 12582912 | tf_op jit(solution)/shard_map/add | solution.py:49
  165.1 11.7 %cholesky.286 = f32[128,128]{1,0:T(8,128)S(1)} custom-call(f32[128,128]{1,0:T(8,128)S(1)} %cholesky.426), custom_call_target="Cholesky" | custom-call | tf_op jit(solution)/shard_map/jit(cholesky)/cholesky | solution.py:32
  176.8 9.8 %custom-call.28 = f32[1,128,128]{1,2,0:T(8,128)S(1)} custom-call(f32[1,128,128]{2,1,0:T(8,128)S(1)} %get-tuple-element.47), custom_call_target="InvertDiagBlocksLowerTriangular" | custom-call | tf_op jit(solution)/shard_map/jit(cholesky)/cholesky | solution.py:32
  187.4 12.2 %cholesky.305 = f32[128,128]{1,0:T(8,128)S(1)} custom-call(f32[128,128]{1,0:T(8,128)S(1)} %cholesky.430), custom_call_target="Cholesky" | custom-call | tf_op jit(solution)/shard_map/jit(cholesky)/cholesky | solution.py:32
  199.7 9.8 %custom-call.29 = f32[1,128,128]{1,2,0:T(8,128)S(1)} custom-call(f32[1,128,128]{2,1,0:T(8,128)S(1)} %get-tuple-element.44), custom_call_target="InvertDiagBlocksLowerTriangular" | custom-call | tf_op jit(solution)/shard_map/jit(cholesky)/cholesky | solution.py:32
  210.1 11.7 %cholesky.326 = f32[128,128]{1,0:T(8,128)S(1)} custom-call(f32[128,128]{1,0:T(8,128)S(1)} %cholesky.435), custom_call_target="Cholesky" | custom-call | tf_op jit(solution)/shard_map/jit(cholesky)/cholesky | solution.py:32
  222.6 9.8 %custom-call.30 = f32[1,128,128]{1,2,0:T(8,128)S(1)} custom-call(f32[1,128,128]{2,1,0:T(8,128)S(1)} %get-tuple-element.41), custom_call_target="InvertDiagBlocksLowerTriangular" | custom-call | tf_op jit(solution)/shard_map/jit(cholesky)/cholesky | solution.py:32
  233.0 11.9 %cholesky.343 = f32[128,128]{1,0:T(8,128)S(1)} custom-call(f32[128,128]{1,0:T(8,128)S(1)} %convolution_subtract_fusion.5), custom_call_target="Cholesky" | custom-call | tf_op jit(solution)/shard_map/jit(cholesky)/cholesky | solution.py:32
  250.1 14.1 %while.1 = (s32[]{:T(128)}, f32[512,512]{1,0:T(8,128)}, s32[4,2]{0,1:T(2,128)S(1)}, f32[4,128,128]{2,1,0:T(8,128)}, s32[]{:T(128)}) while((s32[]{:T(128)}, f32[512,512]{1,0:T(8,128)}, s32[4,2]{0,1:T(2,128)S(1)}, f32[4,128,128]{2,1,0:T(8,128)}, s32[]{:T(128)}) %tuple.36), condition=%wide.while_cond, body=%wide.while_body.sunk | while | flops 2 | bytes 132705 | solution.py:33
  250.7 2.9 bitcast_dynamic-update-slice_fusion.2
  264.2 40.1 %custom-call.24 = f32[4,128,128]{1,2,0:T(8,128)S(1)} custom-call(f32[4,128,128]{2,1,0:T(8,128)} %get-tuple-element.13), custom_call_target="InvertDiagBlocksLowerTriangular" | custom-call | tf_op jit(solution)/shard_map/jit(_solve_triangular)/triangular_solve | solution.py:33
  311.7 3.4 slice_subtract_fusion
  318.9 11.7 %cholesky.358 = f32[128,128]{1,0:T(8,128)S(1)} custom-call(f32[128,128]{1,0:T(8,128)S(1)} %cholesky.439), custom_call_target="Cholesky" | custom-call | tf_op jit(solution)/shard_map/jit(cholesky)/cholesky | solution.py:35
  330.7 9.8 %custom-call.31 = f32[1,128,128]{1,2,0:T(8,128)S(1)} custom-call(f32[1,128,128]{2,1,0:T(8,128)S(1)} %get-tuple-element.37), custom_call_target="InvertDiagBlocksLowerTriangular" | custom-call | tf_op jit(solution)/shard_map/jit(cholesky)/cholesky | solution.py:35
  344.3 11.7 %cholesky.377 = f32[128,128]{1,0:T(8,128)S(1)} custom-call(f32[128,128]{1,0:T(8,128)S(1)} %cholesky.443), custom_call_target="Cholesky" | custom-call | tf_op jit(solution)/shard_map/jit(cholesky)/cholesky | solution.py:35
  357.5 9.8 %custom-call.32 = f32[1,128,128]{1,2,0:T(8,128)S(1)} custom-call(f32[1,128,128]{2,1,0:T(8,128)S(1)} %get-tuple-element.34), custom_call_target="InvertDiagBlocksLowerTriangular" | custom-call | tf_op jit(solution)/shard_map/jit(cholesky)/cholesky | solution.py:35
  369.8 11.7 %cholesky.398 = f32[128,128]{1,0:T(8,128)S(1)} custom-call(f32[128,128]{1,0:T(8,128)S(1)} %cholesky.448), custom_call_target="Cholesky" | custom-call | tf_op jit(solution)/shard_map/jit(cholesky)/cholesky | solution.py:35
  382.2 10.0 %custom-call.33 = f32[1,128,128]{1,2,0:T(8,128)S(1)} custom-call(f32[1,128,128]{2,1,0:T(8,128)S(1)} %get-tuple-element.31), custom_call_target="InvertDiagBlocksLowerTriangular" | custom-call | tf_op jit(solution)/shard_map/jit(cholesky)/cholesky | solution.py:35
  393.7 11.7 %cholesky.415 = f32[128,128]{1,0:T(8,128)S(1)} custom-call(f32[128,128]{1,0:T(8,128)S(1)} %convolution_subtract_fusion.4), custom_call_target="Cholesky" | custom-call | tf_op jit(solution)/shard_map/jit(cholesky)/cholesky | solution.py:35
  411.3 5.3 %copy.15 = f32[1,1024,1024]{2,1,0:T(8,128)} copy(f32[1,1024,1024]{1,2,0:T(8,128)} %fusion) | data formatting | bytes 8388608 | tf_op jit(solution)/shard_map/broadcast_in_dim | solution.py:51
  (85 shorter events, 49.3 us)
Async XLA Ops:
  9.2 50.7 %collective-permute-start = (f32[1024,1024]{0,1:T(8,128)S(1)}, f32[1024,1024]{0,1:T(8,128)S(1)}, u32[]{:S(2)}, u32[]{:S(2)}) collective-permute-start(f32[1024,1024]{0,1:T(8,128)S(1)} %select_add_fusion), channel_id=1, source_target_pairs={{0,1},{1,2},{2,3},{3,4},{4,5},{5,6},{6,7},{7,8},{8,9},{9,10},{10,1... | collective-permute-start | bytes 12582920 | tf_op jit(solution)/shard_map/ppermute | solution.py:10
  62.9 93.8 %collective-permute-start.1 = (f32[1024,1024]{0,1:T(8,128)}, f32[1024,1024]{0,1:T(8,128)}, u32[]{:S(2)}, u32[]{:S(2)}) collective-permute-start(f32[1024,1024]{0,1:T(8,128)} %add.45), channel_id=1, source_target_pairs={{0,2},{1,3},{2,4},{3,5},{4,6},{5,7},{6,8},{7,9},{8,10},{9,11},{10,... | collective-permute-start | bytes 12582920 | tf_op jit(solution)/shard_map/ppermute | solution.py:10
  161.1 2.0 copy-start
  304.3 3.8 copy-start.5
  310.0 1.6 copy-start.2
  310.1 1.5 copy-start.3
  317.9 1.0 copy-start.1
  343.7 0.7 copy-start.4
where the time goes:
time: 423 us; the launch traced here: 417 us
  other arithmetic  213 us (50%)
  waiting for transfers between devices  140 us (33%)
  matrix products  27.2 us (6%)
  local copies, waits for them, and re-layouts  25.7 us (6%)
  between operations  6.88 us (2%)
  starting transfers between devices  4.66 us (1%)
    ppermute x2, waiting for transfers between devices, from_behind(): return lax.ppermute(block, axis, route)  140 us
    another operation x15, other arithmetic, split_cholesky(): tail_block = jnp.linalg.cholesky(trailing)  79.4 us
    another operation x14, other arithmetic, split_cholesky(): lead_block = jnp.linalg.cholesky(matrix[:half, :half])  79.1 us
    another operation x3, other arithmetic, split_cholesky(): jax.scipy.linalg.solve_triangular(lead_block, matrix[half:, :half].T, low...  41.4 us
    another operation x12, local copies, waits for them, and re-layouts  14.1 us
    dot_general x1, matrix products, row_gram(): lax.dot_general(block_rows, block_rows, (((0,), (0,)), ((), ())), preferr...  8.52 us
  transfers between devices with their start and end apart: 2, of which 2 were waited for; matrix products, arithmetic and copies ran while one was open for 0% of the time, Pallas kernels for 0%

commit v1 on v0

v1 whole, which is shorter than its diff:
```python
import jax
import jax.numpy as jnp
from jax import lax
from jax.experimental import pallas as pl
from jax.experimental.pallas import tpu as pltpu
from jax.sharding import PartitionSpec as P


def from_behind(block, axis, distance):
    devices = range(lax.axis_size(axis))
    route = [(i - distance, i) for i in devices if i - distance in devices]
    return lax.ppermute(block, axis, route)


def row_gram(block_rows):
    return lax.dot_general(
        block_rows, block_rows, (((0,), (0,)), ((), ())), preferred_element_type=jnp.float32
    )


def tn(a, b):
    return lax.dot_general(a, b, (((0,), (0,)), ((), ())), preferred_element_type=jnp.float32)

def halves(x):
    hi = x.astype(jnp.bfloat16)
    return hi, (x - hi.astype(jnp.float32)).astype(jnp.bfloat16)

def spread(x):
    return jnp.broadcast_to(x, (8, 128))

def factor_rows(block):
    rows = [block[8 * t:8 * t + 8, :] for t in range(8)]
    sub = lax.broadcasted_iota(jnp.int32, (8, 128), 0)
    done = []
    for s in range(8):
        cols = {t: [spread(rows[t][:, 8 * s + m:8 * s + m + 1]) for m in range(8)] for t in range(s, 8)}
        e = [[spread(cols[s][m][q:q + 1, :]) if q >= m else None for m in range(8)] for q in range(8)]
        r = [spread(rows[s][q:q + 1, :]) for q in range(8)]
        for i in range(8):
            inv = lax.rsqrt(e[i][i])
            low = [e[m][i] * inv if m > i else None for m in range(8)]
            r[i] = r[i] * inv
            for m in range(i + 1, 8):
                for q in range(i + 1, m + 1):
                    e[m][q] = e[m][q] - low[m] * low[q]
                r[m] = r[m] - low[m] * r[i]
            for t in range(s + 1, 8):
                cols[t][i] = cols[t][i] * inv
                for m in range(i + 1, 8):
                    cols[t][m] = cols[t][m] - low[m] * cols[t][i]
                rows[t] = rows[t] - cols[t][i] * r[i]
        out = r[7]
        for q in range(7):
            out = jnp.where(sub == q, r[q], out)
        done.append(out)
    return jnp.concatenate(done, 0)

def cholesky_kernel(w_ref, out_ref, s1, s2):
    n = w_ref.shape[0]
    lane = lax.broadcasted_iota(jnp.int32, (64, 128), 1)
    sub = lax.broadcasted_iota(jnp.int32, (64, 128), 0)
    unit = jnp.where(lane - 64 == sub, 1.0, 0.0).astype(jnp.float32)
    for k in range(n // 128):
        c0 = 128 * k
        panel = w_ref[c0:c0 + 128, c0:]
        if k:
            panel = panel - tn(s1[:384 * k, c0:c0 + 128], s2[:384 * k, c0:])
            out_ref[c0:c0 + 128, :c0] = jnp.zeros((128, c0), jnp.float32)
        for h in range(2):
            p = panel[64 * h:64 * h + 64]
            if h:
                b0 = 384 * k
                p = p - tn(s1[b0:b0 + 192, c0:c0 + 128], s2[b0:b0 + 192, c0:])[64:]
            a = p[:, :128]
            if h:
                a = pltpu.roll(a, 64, 1)
            f = factor_rows(jnp.where(lane < 64, a, unit))
            g = jnp.where(lane < 64, pltpu.roll(f, 64, 1), f)
            ghi, glo = halves(g)
            phi, plo = halves(p)
            both = jnp.dot(jnp.concatenate([ghi, glo], 0), jnp.concatenate([phi, plo], 0), preferred_element_type=jnp.float32)
            r = both[:64] + both[64:]
            r0 = c0 + 64 * h
            head = jnp.where(lane >= sub + 64 * h, r[:, :128], 0.0)
            r = jnp.concatenate([head, r[:, 128:]], 1) if c0 + 128 < n else head
            out_ref[r0:r0 + 64, c0:] = r
            hi, lo = halves(r)
            b = 384 * k + 192 * h
            s1[b:b + 64, c0:] = hi
            s1[b + 64:b + 128, c0:] = hi
            s1[b + 128:b + 192, c0:] = lo
            s2[b:b + 64, c0:] = hi
            s2[b + 64:b + 128, c0:] = lo
            s2[b + 128:b + 192, c0:] = hi

def cholesky(w):
    n = w.shape[0]
    return pl.pallas_call(
        cholesky_kernel,
        out_shape=jax.ShapeDtypeStruct((n, n), jnp.float32),
        in_specs=[pl.BlockSpec(memory_space=pltpu.VMEM)],
        out_specs=pl.BlockSpec(memory_space=pltpu.VMEM),
        scratch_shapes=[pltpu.VMEM((3 * n, n), jnp.bfloat16), pltpu.VMEM((3 * n, n), jnp.bfloat16)],
        compiler_params=pltpu.CompilerParams(vmem_limit_bytes=48 << 20),
    )(w)


def body(observations, counts, prior):
    capacity, columns = observations.shape
    live_count = counts[0]
    row_index = lax.broadcasted_iota(jnp.int32, (capacity, 1), 0)
    masked = jnp.where(row_index < live_count, observations, jnp.zeros_like(observations))
    gram_matrix = row_gram(masked)
    gram_matrix = gram_matrix + jnp.diag(prior[0])
    level_one = gram_matrix + from_behind(gram_matrix, "tm", 1)
    level_two = level_one + from_behind(level_one, "tm", 2)
    upper_factor = cholesky(level_two)
    return upper_factor[None]


def solution(mesh):
    placed = (P(("grp", "tm"), None), P(("grp", "tm")), P(("grp", "tm"), None))
    return jax.shard_map(
        body, mesh=mesh, in_specs=placed, out_specs=P(("grp", "tm"), None, None), check_vma=False
    )
```

time: 423 us -> 195 us (0.46); the launches traced: 417 us -> 194 us
  other arithmetic: 213 us -> 2.3 us
  Pallas kernels: 0 us -> 38.9 us
  local copies, waits for them, and re-layouts: 25.7 us -> 0 us
  matrix products: 27.2 us -> 8.37 us
  between operations: 6.88 us -> 0.69 us
    another operation x32 -> x0, other arithmetic: 200 us -> none  [the longest x15 79.4 us: split_cholesky(): tail_block = jnp.linalg.cholesky(trailing)]
    pallas_call x0 -> x1, Pallas kernels: none -> 38.9 us  [cholesky(): pl.pallas_call(cholesky_kernel, out_shape=jax.ShapeDtypeStruct((n, n), jn...]
    another operation x19 -> x0, matrix products: 15.3 us -> none  [the longest x7 6.82 us: split_cholesky(): jax.scipy.linalg.solve_triangular(lead_block, matrix[half:, :half].T, low...]
    another operation x26 -> x0, local copies, waits for them, and re-layouts: 14.9 us -> none
    broadcast_in_dim x1 -> x0, local copies, waits for them, and re-layouts: 5.34 us -> none  [body(): return upper_factor[None]]
where the time goes in v1:
time: 195 us; the launch traced here: 194 us
  waiting for transfers between devices  140 us (72%)
  Pallas kernels  38.9 us (20%)
  matrix products  8.37 us (4%)
  starting transfers between devices  4.63 us (2%)
  other arithmetic  2.3 us (1%)
    ppermute x2, waiting for transfers between devices, from_behind(): return lax.ppermute(block, axis, route)  140 us
    pallas_call x1, Pallas kernels, cholesky(): pl.pallas_call(cholesky_kernel, out_shape=jax.ShapeDtypeStruct((n, n), jn...  38.9 us
    dot_general x1, matrix products, row_gram(): lax.dot_general(block_rows, block_rows, (((0,), (0,)), ((), ())), preferr...  8.37 us
    ppermute x2, starting transfers between devices, from_behind(): return lax.ppermute(block, axis, route)  4.63 us
  transfers between devices with their start and end apart: 2, of which 2 were waited for; matrix products, arithmetic and copies ran while one was open for 0% of the time, Pallas kernels for 0%

profile of v1, /device:TPU:24, one launch (start us, length us, event | category | flops | bytes accessed | tf_op | source)
XLA Modules:
  0.0 194.5 jit_solution(5843958809261950576)
XLA Ops:
  0.7 8.4 %select_add_fusion = f32[1024,1024]{1,0:T(8,128)S(1)} fusion(f32[1024]{0:T(1024)} %bitcast.4, bf16[2048,1024]{1,0:T(8,128)(2,1)} %param.3, pred[2048]{0:T(1024)(128)(4,1)S(1)} %iota_compare_fusion.1), kind=kOutput, calls=%fused_computation | convolution fusion | flops 4300210176 | bytes 8394752 | tf_op jit(solution)/shard_map/dot_general | solution.py:16
  9.0 1.9 collective-permute-start
  11.0 48.8 %collective-permute-done = f32[1024,1024]{1,0:T(8,128)S(1)} collective-permute-done((f32[1024,1024]{1,0:T(8,128)S(1)}, f32[1024,1024]{1,0:T(8,128)S(1)}, u32[]{:S(2)}, u32[]{:S(2)}) %collective-permute-start) | collective-permute-done | bytes 4194336 | tf_op jit(solution)/shard_map/ppermute | solution.py:12
  59.8 1.4 add.10
  61.1 2.7 %collective-permute-start.1 = (f32[1024,1024]{1,0:T(8,128)S(1)}, f32[1024,1024]{1,0:T(8,128)S(1)}, u32[]{:S(2)}, u32[]{:S(2)}) collective-permute-start(f32[1024,1024]{1,0:T(8,128)S(1)} %add.10), channel_id=1, source_target_pairs={{0,2},{1,3},{2,4},{3,5},{4,6},{5,7},{6,8},{7,9},{8,10},{9,11},{10,... | collective-permute-start | bytes 12582920 | tf_op jit(solution)/shard_map/ppermute | solution.py:12
  63.8 90.8 %collective-permute-done.1 = f32[1024,1024]{1,0:T(8,128)S(1)} collective-permute-done((f32[1024,1024]{1,0:T(8,128)S(1)}, f32[1024,1024]{1,0:T(8,128)S(1)}, u32[]{:S(2)}, u32[]{:S(2)}) %collective-permute-start.1) | collective-permute-done | bytes 4194336 | tf_op jit(solution)/shard_map/ppermute | solution.py:12
  154.7 0.9 add.11.w_ref
  155.6 38.9 %shard_map.37 = f32[1024,1024]{1,0:T(8,128)} custom-call(f32[1024,1024]{1,0:T(8,128)S(1)} %add.11.w_ref), custom_call_target="tpu_custom_call" | custom-call | tf_op jit(solution)/shard_map/pallas_call | solution.py:98
  (1 shorter events, 0.0 us)
Async XLA Ops:
  9.0 50.7 %collective-permute-start = (f32[1024,1024]{1,0:T(8,128)S(1)}, f32[1024,1024]{1,0:T(8,128)S(1)}, u32[]{:S(2)}, u32[]{:S(2)}) collective-permute-start(f32[1024,1024]{1,0:T(8,128)S(1)} %select_add_fusion), channel_id=1, source_target_pairs={{0,1},{1,2},{2,3},{3,4},{4,5},{5,6},{6,7},{7,8},{8,9},{9,10},{10,1... | collective-permute-start | bytes 12582920 | tf_op jit(solution)/shard_map/ppermute | solution.py:12
  61.1 93.5 %collective-permute-start.1 = (f32[1024,1024]{1,0:T(8,128)S(1)}, f32[1024,1024]{1,0:T(8,128)S(1)}, u32[]{:S(2)}, u32[]{:S(2)}) collective-permute-start(f32[1024,1024]{1,0:T(8,128)S(1)} %add.10), channel_id=1, source_target_pairs={{0,2},{1,3},{2,4},{3,5},{4,6},{5,7},{6,8},{7,9},{8,10},{9,11},{10,... | collective-permute-start | bytes 12582920 | tf_op jit(solution)/shard_map/ppermute | solution.py:12

commit v2 on v1

--- a/solution.py
+++ b/solution.py
@@ -1,21 +1,10 @@
+import functools
 import jax
 import jax.numpy as jnp
 from jax import lax
 from jax.experimental import pallas as pl
 from jax.experimental.pallas import tpu as pltpu
 from jax.sharding import PartitionSpec as P
-
-
-def from_behind(block, axis, distance):
-    devices = range(lax.axis_size(axis))
-    route = [(i - distance, i) for i in devices if i - distance in devices]
-    return lax.ppermute(block, axis, route)
-
-
-def row_gram(block_rows):
-    return lax.dot_general(
-        block_rows, block_rows, (((0,), (0,)), ((), ())), preferred_element_type=jnp.float32
-    )
 
 
 def tn(a, b):
@@ -55,14 +44,141 @@
         done.append(out)
     return jnp.concatenate(done, 0)
 
-def cholesky_kernel(w_ref, out_ref, s1, s2):
-    n = w_ref.shape[0]
+
+def window_kernel(steps, h_ref, count_ref, prior_ref, out_ref, gram, pair, near, behind, far, s1, s2,
+                  send_gram, send_pair, send_on, got_near, got_behind, got_far):
+    n = out_ref.shape[0]
+    panels = n // 128
+    t = lax.axis_index("tm")
+    odd = lax.rem(t, 2) == 1
+    even = jnp.logical_not(odd)
+
+    def cut(ref, k):
+        return ref.at[pl.ds(128 * k, 128), pl.ds(128 * k, n - 128 * k)]
+
+    def copy(k, src, dst, send, recv, target):
+        return pltpu.make_async_remote_copy(
+            src_ref=cut(src, k), dst_ref=cut(dst, k), send_sem=send.at[k], recv_sem=recv.at[k],
+            device_id={"tm": target}, device_id_type=pl.DeviceIdType.MESH)
+
+    def gram_to_pair(k):
+        return copy(k, gram, near, send_gram, got_near, t + 1)
+
+    def gram_ahead(k):
+        return copy(k, gram, far, send_gram, got_far, t + 3)
+
+    def pair_ahead(k):
+        return copy(k, pair, behind, send_pair, got_behind, t + 2)
+
+    def pass_on(k):
+        return copy(k, behind, behind, send_on, got_behind, t - 1)
+
+    barrier = pltpu.get_barrier_semaphore()
+
+    def greet(target):
+        pl.semaphore_signal(barrier, inc=1, device_id={"tm": target}, device_id_type=pl.DeviceIdType.MESH)
+
+    @pl.when(odd)
+    def _():
+        greet(t - 1)
+
+        @pl.when(t >= 2)
+        def _():
+            greet(t - 2)
+
+        @pl.when(t + 3 < steps)
+        def _():
+            pl.semaphore_wait(barrier, 3)
+
+        @pl.when(t + 3 == steps)
+        def _():
+            pl.semaphore_wait(barrier, 2)
+
+        @pl.when(t + 1 == steps)
+        def _():
+            pl.semaphore_wait(barrier, 1)
+
+    @pl.when(even)
+    def _():
+        greet(t + 1)
+
+        @pl.when(t >= 3)
+        def _():
+            greet(t - 3)
+
+        pl.semaphore_wait(barrier, 1)
+
+    count = count_ref[0]
+    live = lax.broadcasted_iota(jnp.int32, (h_ref.shape[0], 128), 0) < count
+    eye = lax.broadcasted_iota(jnp.int32, (128, 128), 0) == lax.broadcasted_iota(jnp.int32, (128, 128), 1)
+    def add_pair(k):
+        @pl.when(odd)
+        def _():
+            at = (slice(128 * k, 128 * k + 128), slice(128 * k, n))
+            gram_to_pair(k).wait_recv()
+            pair[at] = gram[at] + near[at]
+
+            @pl.when(t + 2 < steps)
+            def _():
+                pair_ahead(k).start()
+
+    for k in range(panels):
+        c0 = 128 * k
+        rows = h_ref[:, c0:c0 + 128]
+        rows = jnp.where(live, rows, jnp.zeros_like(rows))
+        g = tn(rows, h_ref[:, c0:])
+        lead = g[:, :128] + jnp.where(eye, prior_ref[:, c0:c0 + 128], 0.0)
+        gram[c0:c0 + 128, c0:c0 + 128] = lead
+        if k + 1 < panels:
+            gram[c0:c0 + 128, c0 + 128:] = g[:, 128:]
+
+        @pl.when(even)
+        def _():
+            gram_to_pair(k).start()
+
+        @pl.when(odd & (t + 3 < steps))
+        def _():
+            gram_ahead(k).start()
+
+        if k:
+            add_pair(k - 1)
+
+    add_pair(panels - 1)
+
     lane = lax.broadcasted_iota(jnp.int32, (64, 128), 1)
     sub = lax.broadcasted_iota(jnp.int32, (64, 128), 0)
     unit = jnp.where(lane - 64 == sub, 1.0, 0.0).astype(jnp.float32)
-    for k in range(n // 128):
+    for k in range(panels):
         c0 = 128 * k
-        panel = w_ref[c0:c0 + 128, c0:]
+        at = (slice(c0, c0 + 128), slice(c0, n))
+
+        @pl.when(t >= 2)
+        def _():
+            pair_ahead(k).wait_recv()
+
+        @pl.when(odd & (t >= 2))
+        def _():
+            pass_on(k).start()
+            out_ref[at] = pair[at] + behind[at]
+
+        @pl.when(odd & (t < 2))
+        def _():
+            out_ref[at] = pair[at]
+
+        @pl.when(even & (t < 2))
+        def _():
+            out_ref[at] = gram[at]
+
+        @pl.when(even & (t == 2))
+        def _():
+            out_ref[at] = gram[at] + behind[at]
+
+        @pl.when(even & (t >= 3))
+        def _():
+            gram_ahead(k).wait_recv()
+            out_ref[at] = gram[at] + behind[at] + far[at]
+
+        panel = out_ref[at]
         if k:
             panel = panel - tn(s1[:384 * k, c0:c0 + 128], s2[:384 * k, c0:])
             out_ref[c0:c0 + 128, :c0] = jnp.zeros((128, c0), jnp.float32)
@@ -93,29 +209,40 @@
             s2[b + 64:b + 128, c0:] = lo
             s2[b + 128:b + 192, c0:] = hi
 
-def cholesky(w):
-    n = w.shape[0]
-    return pl.pallas_call(
-        cholesky_kernel,
+    for k in range(panels):
+        @pl.when(even)
+        def _():
+            gram_to_pair(k).wait_send()
+
+        @pl.when(odd & (t + 3 < steps))
+        def _():
+            gram_ahead(k).wait_send()
+
+        @pl.when(odd & (t + 2 < steps))
+        def _():
+            pair_ahead(k).wait_send()
+
+        @pl.when(odd & (t >= 2))
+        def _():
+            pass_on(k).wait_send()
+
+
+def body(observations, counts, prior):
+    n = observations.shape[1]
+    panels = n // 128
+    full = pltpu.VMEM((n, n), jnp.float32)
+    factor = pl.pallas_call(
+        functools.partial(window_kernel, lax.axis_size("tm")),
         out_shape=jax.ShapeDtypeStruct((n, n), jnp.float32),
-        in_specs=[pl.BlockSpec(memory_space=pltpu.VMEM)],
+        in_specs=[pl.BlockSpec(memory_space=pltpu.VMEM), pl.BlockSpec(memory_space=pltpu.SMEM),
+                  pl.BlockSpec(memory_space=pltpu.VMEM)],
         out_specs=pl.BlockSpec(memory_space=pltpu.VMEM),
-        scratch_shapes=[pltpu.VMEM((3 * n, n), jnp.bfloat16), pltpu.VMEM((3 * n, n), jnp.bfloat16)],
-        compiler_params=pltpu.CompilerParams(vmem_limit_bytes=48 << 20),
-    )(w)
-
-
-def body(observations, counts, prior):
-    capacity, columns = observations.shape
-    live_count = counts[0]
-    row_index = lax.broadcasted_iota(jnp.int32, (capacity, 1), 0)
-    masked = jnp.where(row_index < live_count, observations, jnp.zeros_like(observations))
-    gram_matrix = row_gram(masked)
-    gram_matrix = gram_matrix + jnp.diag(prior[0])
-    level_one = gram_matrix + from_behind(gram_matrix, "tm", 1)
-    level_two = level_one + from_behind(level_one, "tm", 2)
-    upper_factor = cholesky(level_two)
-    return upper_factor[None]
+        scratch_shapes=[full] * 5 + [pltpu.VMEM((3 * n, n), jnp.bfloat16)] * 2
+        + [pltpu.SemaphoreType.DMA((panels,))] * 6,
+        compiler_params=pltpu.CompilerParams(
+            collective_id=0, has_side_effects=True, vmem_limit_bytes=56 << 20),
+    )(observations, counts, prior)
+    return factor[None]
 
 
 def solution(mesh):

time: 195 us -> 79.5 us (0.41)
  waiting for transfers between devices: 140 us -> 0 us
  Pallas kernels: 38.9 us -> 73.9 us
  matrix products: 8.37 us -> 0 us
  local copies, waits for them, and re-layouts: 0 us -> 4.79 us
  starting transfers between devices: 4.63 us -> 0 us
  other arithmetic: 2.3 us -> 0 us
    ppermute x2 -> x0, waiting for transfers between devices: 140 us -> none  [from_behind(): return lax.ppermute(block, axis, route)]
    pallas_call x1, Pallas kernels: 38.9 us -> 73.9 us  [body(): pl.pallas_call(functools.partial(window_kernel, lax.axis_size('tm')), out...]
    dot_general x1 -> x0, matrix products: 8.37 us -> none  [row_gram(): lax.dot_general(block_rows, block_rows, (((0,), (0,)), ((), ())), preferr...]
    unnamed x0 -> x1, local copies, waits for them, and re-layouts: none -> 4.79 us
    ppermute x2 -> x0, starting transfers between devices: 4.63 us -> none  [from_behind(): return lax.ppermute(block, axis, route)]
    add x2 -> x0, other arithmetic: 2.29 us -> none  [the longest x1 1.36 us: body(): level_one = gram_matrix + from_behind(gram_matrix, 'tm', 1)]
  transfers between devices with their start and end apart: 2 -> 0, of which waited for: 2 -> 0; matrix products, arithmetic and copies ran while one was open for 0% -> 0% of each run, Pallas kernels for 0% -> 0%
where the time goes in v2:
time: 79.5 us; the launch traced here: 79.3 us
  Pallas kernels  73.9 us (93%)
  local copies, waits for them, and re-layouts  4.79 us (6%)
    pallas_call x1, Pallas kernels, body(): pl.pallas_call(functools.partial(window_kernel, lax.axis_size('tm')), out...  73.9 us
    unnamed x1, local copies, waits for them, and re-layouts  4.79 us

profile of v2, /device:TPU:24, one launch (start us, length us, event | category | flops | bytes accessed | tf_op | source)
XLA Modules:
  0.0 79.3 jit_solution(9990134527032401697)
XLA Ops:
  0.7 73.9 %shard_map.37 = f32[1024,1024]{1,0:T(8,128)} custom-call(bf16[2048,1024]{1,0:T(8,128)(2,1)} %h_ref.1, s32[1]{0:T(128)S(6)} %copy.5.count_ref, f32[1,1024]{1,0:T(1,128)} %prior_ref.1), custom_call_target="tpu_custom_call" | custom-call | tf_op jit(solution)/shard_map/pallas_call | solution.py:234
  74.6 4.8 %copy.6 = f32[1,1024,1024]{2,1,0:T(8,128)} copy(f32[1,1024,1024]{2,1,0:T(8,128)} %bitcast.1) | data formatting | bytes 8388608

commit v3 on v2

--- a/solution.py
+++ b/solution.py
@@ -45,8 +45,9 @@
     return jnp.concatenate(done, 0)
 
 
-def window_kernel(steps, h_ref, count_ref, prior_ref, out_ref, gram, pair, near, behind, far, s1, s2,
-                  send_gram, send_pair, send_on, got_near, got_behind, got_far):
+def window_kernel(steps, h_ref, count_ref, prior_ref, out_ref, gram, pair, near, behind, far, relay, s1, s2,
+                  send_gram, send_pair, send_on, got_near, got_behind, got_far,
+                  send_off, got_relay):
     n = out_ref.shape[0]
     panels = n // 128
     t = lax.axis_index("tm")
@@ -73,6 +74,16 @@
     def pass_on(k):
         return copy(k, behind, behind, send_on, got_behind, t - 1)
 
+    third = lax.rem(t, 4) == 3
+    via = third & (t + 4 < steps)
+    carries = third & (t >= 4)
+
+    def relay_out(k):
+        return copy(k, pair, relay, send_pair, got_relay, t + 4)
+
+    def relay_on(k):
+        return copy(k, relay, behind, send_off, got_behind, t - 2)
+
     barrier = pltpu.get_barrier_semaphore()
 
     def greet(target):
@@ -86,17 +97,24 @@
         def _():
             greet(t - 2)
 
-        @pl.when(t + 3 < steps)
-        def _():
-            pl.semaphore_wait(barrier, 3)
-
-        @pl.when(t + 3 == steps)
-        def _():
-            pl.semaphore_wait(barrier, 2)
-
-        @pl.when(t + 1 == steps)
-        def _():
-            pl.semaphore_wait(barrier, 1)
+        @pl.when(carries)
+        def _():
+            greet(t - 4)
+
+        @pl.when((lax.rem(t, 4) == 1) & (t >= 5) & (t + 2 < steps))
+        def _():
+            greet(t + 2)
+
+        targets = {}
+        for v in range(1, steps, 2):
+            number = 1 + (v + 2 < steps) + (v + 3 < steps)
+            if v % 4 == 3:
+                number += (v + 4 < steps) + (v >= 4)
+            targets.setdefault(number, []).append(t == v)
+        for number, cases in targets.items():
+            @pl.when(functools.reduce(jnp.logical_or, cases))
+            def _():
+                pl.semaphore_wait(barrier, number)
 
     @pl.when(even)
     def _():
@@ -118,9 +136,18 @@
             gram_to_pair(k).wait_recv()
             pair[at] = gram[at] + near[at]
 
-            @pl.when(t + 2 < steps)
-            def _():
-                pair_ahead(k).start()
+            if k % 2:
+                @pl.when(via)
+                def _():
+                    relay_out(k).start()
+
+                @pl.when(jnp.logical_not(via) & (t + 2 < steps))
+                def _():
+                    pair_ahead(k).start()
+            else:
+                @pl.when(t + 2 < steps)
+                def _():
+                    pair_ahead(k).start()
 
     for k in range(panels):
         c0 = 128 * k
@@ -151,6 +178,12 @@
     for k in range(panels):
         c0 = 128 * k
         at = (slice(c0, c0 + 128), slice(c0, n))
+
+        if k % 2:
+            @pl.when(carries)
+            def _():
+                relay_out(k).wait_recv()
+                relay_on(k).start()
 
         @pl.when(t >= 2)
         def _():
@@ -226,6 +259,11 @@
         def _():
             pass_on(k).wait_send()
 
+        if k % 2:
+            @pl.when(carries)
+            def _():
+                relay_on(k).wait_send()
+
 
 def body(observations, counts, prior):
     n = observations.shape[1]
@@ -237,8 +275,8 @@
         in_specs=[pl.BlockSpec(memory_space=pltpu.VMEM), pl.BlockSpec(memory_space=pltpu.SMEM),
                   pl.BlockSpec(memory_space=pltpu.VMEM)],
         out_specs=pl.BlockSpec(memory_space=pltpu.VMEM),
-        scratch_shapes=[full] * 5 + [pltpu.VMEM((3 * n, n), jnp.bfloat16)] * 2
-        + [pltpu.SemaphoreType.DMA((panels,))] * 6,
+        scratch_shapes=[full] * 6 + [pltpu.VMEM((3 * n, n), jnp.bfloat16)] * 2
+        + [pltpu.SemaphoreType.DMA((panels,))] * 8,
         compiler_params=pltpu.CompilerParams(
             collective_id=0, has_side_effects=True, vmem_limit_bytes=56 << 20),
     )(observations, counts, prior)

time: 79.5 us -> 87.2 us (1.097)
  Pallas kernels: 73.9 us -> 81.6 us
    pallas_call x1, Pallas kernels: 73.9 us -> 81.6 us  [body(): pl.pallas_call(functools.partial(window_kernel, lax.axis_size('tm')), out...]
where the time goes in v3:
time: 87.2 us; the launch traced here: 87.1 us
  Pallas kernels  81.6 us (94%)
  local copies, waits for them, and re-layouts  4.79 us (5%)
    pallas_call x1, Pallas kernels, body(): pl.pallas_call(functools.partial(window_kernel, lax.axis_size('tm')), out...  81.6 us
    unnamed x1, local copies, waits for them, and re-layouts  4.79 us

profile of v3, /device:TPU:24, one launch (start us, length us, event | category | flops | bytes accessed | tf_op | source)
XLA Modules:
  0.0 87.1 jit_solution(12060351120936946431)
XLA Ops:
  0.7 81.6 %shard_map.37 = f32[1024,1024]{1,0:T(8,128)} custom-call(bf16[2048,1024]{1,0:T(8,128)(2,1)} %h_ref.1, s32[1]{0:T(128)S(6)} %copy.5.count_ref, f32[1,1024]{1,0:T(1,128)} %prior_ref.1), custom_call_target="tpu_custom_call" | custom-call | tf_op jit(solution)/shard_map/pallas_call | solution.py:272
  82.3 4.8 %copy.6 = f32[1,1024,1024]{2,1,0:T(8,128)} copy(f32[1,1024,1024]{2,1,0:T(8,128)} %bitcast.1) | data formatting | bytes 8388608
